TPU v7x, 32 devices: a whole 2x2x4 slice. The times are simulated.
32 devices in a mesh: groups: 2 (over x), dp: 16 (over z, y, core).
Axes of the slice: x: 2, y: 2, z: 4, core: 2. Of those that a mesh axis runs over, the one named last changes fastest.
Arguments:
- acts: bfloat16 [12288, 8192], P(('groups', 'dp')), parts along dimension 0, may hold values from -6 to 6
- grad_out: bfloat16 [12288, 1024], P(('groups', 'dp')), parts along dimension 0, may hold values from -0.29882812 to 0.29882812
- low_acts: bfloat16 [12288, 64], P(('groups', 'dp')), parts along dimension 0, may hold values from -6 to 6
- up_weight: bfloat16 [64, 64, 1024], P('dp'), may hold values from -0.1875 to 0.1875
- block_adapter: int32 [96], P('groups'), parts along dimension 0, may hold values from 0 to 63
- block_fill: int32 [96], P(('groups', 'dp')), parts along dimension 0, may hold values from 32 to 128
- owner_slot: int32 [64], replicated, may hold values from 0 to 63, each once
Outputs:
- grad_down: bfloat16 [128, 64, 8192], P(('groups', 'dp')), parts along dimension 0
- grad_up: bfloat16 [128, 64, 1024], P(('groups', 'dp')), parts along dimension 0
There are 2 independent parts, one for each index of `groups`. A program takes and returns all parts, laid end to end along the dimension named above; an argument that names none is the same for every part. Nothing has to cross between parts.
All inputs are finite; a program needn't handle non-finite values.
Results may differ from a plain program's by a relative error of at most 0.0049.
Values may be sent and summed in bfloat16 or wider, within the bound.
No kernel may reach another device: no remote copies, remote signals or barrier semaphores. Data moves between devices by JAX's collectives and lax.ppermute only.
A program may use at most 128 MiB of HBM per device.

v0:
```python
import functools

import jax
import jax.numpy as jnp
from jax import lax
from jax.experimental import pallas as pl
from jax.experimental.pallas import tpu as pltpu
from jax.sharding import PartitionSpec as P

BLOCK = 128
SCALE = 2.0
CHUNKS = 2
PARTS_A_STEP = 4
GROUPS = 8
BF16 = jnp.bfloat16
F32 = jnp.float32
VMEM_LIMIT = 48 * 1024 * 1024
SMALL, LARGE = 1 << 20, 1 << 38


def params():
    return pltpu.CompilerParams(vmem_limit_bytes=VMEM_LIMIT)


def spec():
    return pl.BlockSpec(memory_space=pltpu.VMEM)


def pick_kernel(slot_ref, parts_ref, out_ref):
    def step(b, carry):
        out_ref[b] = parts_ref[slot_ref[b]]
        return carry

    lax.fori_loop(0, out_ref.shape[0], step, 0)


def pick(slot_of, parts):
    blocks = slot_of.shape[0]
    return pl.pallas_call(
        pick_kernel,
        out_shape=jax.ShapeDtypeStruct((blocks,) + parts.shape[1:], BF16),
        in_specs=[pl.BlockSpec(memory_space=pltpu.SMEM), spec()],
        out_specs=spec(),
        compiler_params=params(),
    )(slot_of, parts)


def rank_kernel(lane_groups, fill_ref, parts_ref, grad_ref, *refs):
    out_ref, weight = refs[-2:]
    parts, blocks, rows, lanes = parts_ref.shape
    for b in range(blocks):
        for p in range(parts):
            g, l = p // lane_groups, p % lane_groups
            weight[b, g * rows : (g + 1) * rows, l * lanes : (l + 1) * lanes] = parts_ref[p, b]
    for b in range(blocks):
        turned = SCALE * lax.dot_general(
            weight[b],
            grad_ref[b * BLOCK : (b + 1) * BLOCK, :],
            (((1,), (1,)), ((), ())),
            preferred_element_type=F32,
        )
        live = lax.broadcasted_iota(jnp.int32, turned.shape, 1) < fill_ref[b]
        out_ref[b] = jnp.where(live, turned, 0.0).astype(BF16)


def rank_cotangent(fill, parts, grad, lane_groups, rank, after):
    blocks = fill.shape[0]
    return pl.pallas_call(
        functools.partial(rank_kernel, lane_groups),
        out_shape=jax.ShapeDtypeStruct((blocks, rank, BLOCK), BF16),
        in_specs=[pl.BlockSpec(memory_space=pltpu.SMEM), spec(), spec()]
        + [pl.BlockSpec(memory_space=pl.ANY)] * len(after),
        out_specs=spec(),
        scratch_shapes=[pltpu.VMEM((blocks, rank, grad.shape[1]), BF16)],
        compiler_params=params(),
    )(fill, parts, grad, *after)


def up_kernel(fill_ref, low_ref, grad_ref, out_ref):
    parts, blocks, rank, width = out_ref.shape
    for b in range(blocks):
        low = low_ref[:, b * BLOCK : (b + 1) * BLOCK].astype(F32)
        live = lax.broadcasted_iota(jnp.int32, low.shape, 1) < fill_ref[b]
        low = jnp.where(live, low, 0.0).astype(BF16)
        whole = SCALE * jnp.dot(
            low, grad_ref[b * BLOCK : (b + 1) * BLOCK, :], preferred_element_type=F32
        )
        for p in range(parts):
            out_ref[p, b] = whole[:, p * width : (p + 1) * width].astype(BF16)


def up_products(fill, low_t, grad, parts):
    blocks, rank = fill.shape[0], low_t.shape[0]
    return pl.pallas_call(
        up_kernel,
        out_shape=jax.ShapeDtypeStruct((parts, blocks, rank, grad.shape[1] // parts), BF16),
        in_specs=[pl.BlockSpec(memory_space=pltpu.SMEM), spec(), spec()],
        out_specs=spec(),
        compiler_params=params(),
    )(fill, low_t, grad)


def down_kernel(low_ref, acts_ref, out_ref):
    parts, blocks, _, width = out_ref.shape
    for p in range(parts):
        for b in range(blocks):
            out_ref[p, b] = jnp.dot(
                low_ref[b],
                acts_ref[b * BLOCK : (b + 1) * BLOCK, p * width : (p + 1) * width],
                preferred_element_type=F32,
            ).astype(BF16)


def products(low_t, acts, parts, chunk):
    blocks, rank, _ = low_t.shape
    rows, width = acts.shape[0], acts.shape[1] // (parts * CHUNKS)
    steps = max(parts // PARTS_A_STEP, 1)
    each = parts // steps
    return pl.pallas_call(
        down_kernel,
        grid=(steps,),
        out_shape=jax.ShapeDtypeStruct((parts, blocks, rank, width), BF16),
        in_specs=[
            pl.BlockSpec(low_t.shape, lambda p: (0, 0, 0)),
            pl.BlockSpec((rows, width * each), lambda p: (0, chunk * steps + p)),
        ],
        out_specs=pl.BlockSpec((each, blocks, rank, width), lambda p: (p, 0, 0, 0)),
        compiler_params=params(),
        cost_estimate=pl.CostEstimate(
            flops=2 * rows * rank * width * parts,
            bytes_accessed=2 * parts * width * (rows + blocks * rank),
            transcendentals=0,
        ),
    )(low_t, acts)


def sum_kernel(blocks, count, has_extra, outs, groups, table_ref, *refs):
    held = refs[:count]
    if groups:
        kept, sems = refs[-2:]
        refs = refs[:-2]
    dests = refs[-outs:]
    outs = dests
    if groups:
        size = kept.shape[0] // groups
        outs = [kept.at[pl.ds(n * size, size)] for n in range(groups)]
        if len(dests) == 1:
            dests = [dests[0].at[pl.ds(n * size, size)] for n in range(groups)]
    copies = []
    extra_ref = refs[count] if has_extra else None
    targets = sum(out.shape[0] for out in outs)
    rank = outs[0].shape[1]
    base = blocks * count

    for n, out_ref in enumerate(outs):
        shift = n * out_ref.shape[0]

        def step(m, carry, out_ref=out_ref, shift=shift):
            at = base + shift + m
            low = 0
            for i, held_ref in enumerate(held):
                high = low + held_ref.shape[2]

                def add(j, total, i=i, held_ref=held_ref):
                    return total + held_ref[table_ref[i * blocks + j]].astype(F32)

                def add_extra(j, total, low=low, high=high):
                    return total + extra_ref[j, :, low:high].astype(F32)

                zero = jnp.zeros((rank, high - low), F32)
                total = lax.fori_loop(table_ref[at], table_ref[at + targets], add, zero)
                if has_extra:
                    total = lax.fori_loop(
                        table_ref[at + 2 * targets], table_ref[at + 3 * targets], add_extra, total
                    )
                out_ref[m, :, low:high] = total.astype(BF16)
                low = high
            return carry

        lax.fori_loop(0, out_ref.shape[0], step, 0)
        if groups:
            copies.append(pltpu.make_async_copy(out_ref, dests[n], sems.at[n]))
            copies[-1].start()
    for copy in copies:
        copy.wait()


def slot_sums(table, held, targets, hint, extra=None, outs=1, after=(), groups=0):
    blocks, rank, _ = held[0].shape
    width = sum(x.shape[2] for x in held)
    operands = list(held) + ([] if extra is None else [extra])
    shape = jax.ShapeDtypeStruct((targets // outs, rank, width), BF16)
    return pl.pallas_call(
        functools.partial(sum_kernel, blocks, len(held), extra is not None, outs, groups),
        out_shape=[shape] * outs,
        in_specs=[pl.BlockSpec(memory_space=pltpu.SMEM)]
        + [spec()] * len(operands)
        + [pl.BlockSpec(memory_space=pl.ANY)] * len(after),
        out_specs=[pl.BlockSpec(memory_space=pltpu.HBM) if groups else spec()] * outs,
        scratch_shapes=[
            pltpu.VMEM((targets, rank, width), BF16),
            pltpu.SemaphoreType.DMA((groups,)),
        ]
        if groups
        else [],
        compiler_params=params(),
        cost_estimate=pl.CostEstimate(flops=hint, bytes_accessed=hint, transcendentals=0),
    )(table, *operands, *after)


def place_kernel(*refs):
    landing_ref, got_ref, out_ref = refs[0], refs[1], refs[-1]
    for n in range(out_ref.shape[0]):
        spot = landing_ref[n]
        value = got_ref[0, jnp.maximum(spot, 0)]
        out_ref[n] = jnp.where(spot >= 0, value, jnp.zeros_like(value))


def place_all_kernel(got_ref, *refs):
    refs[-1][...] = got_ref[0]


def place(got, landing, slots, width, column, columns, chunk, into=None):
    parts, held, rank, _ = got.shape
    operands = [got] if landing is None else [landing, got]
    specs = [pl.BlockSpec((1, held, rank, width), lambda p: (p, 0, 0, column))]
    if landing is not None:
        specs = [pl.BlockSpec(memory_space=pltpu.SMEM)] + specs
    if into is not None:
        operands.append(into)
        specs.append(pl.BlockSpec(memory_space=pl.ANY))
    return pl.pallas_call(
        place_all_kernel if landing is None else place_kernel,
        grid=(parts,),
        out_shape=jax.ShapeDtypeStruct((slots, rank, columns), BF16),
        in_specs=specs,
        out_specs=pl.BlockSpec((slots, rank, width), lambda p: (0, 0, chunk * parts + p)),
        input_output_aliases={} if into is None else {len(operands) - 1: 0},
        compiler_params=params(),
        cost_estimate=pl.CostEstimate(
            flops=0, bytes_accessed=4 * parts * slots * rank * width, transcendentals=0
        ),
    )(*operands)


def lay_kernel(first, got_ref, _, out_ref, sems):
    parts, _, _, width = got_ref.shape
    copies = [
        pltpu.make_async_copy(
            got_ref.at[p], out_ref.at[:, :, pl.ds((first + p) * width, width)], sems.at[p]
        )
        for p in range(parts)
    ]
    for copy in copies:
        copy.start()
    for copy in copies:
        copy.wait()


def lay(got, first, into):
    anywhere = pl.BlockSpec(memory_space=pl.ANY)
    return pl.pallas_call(
        functools.partial(lay_kernel, first),
        out_shape=jax.ShapeDtypeStruct(into.shape, BF16),
        in_specs=[anywhere, anywhere],
        out_specs=anywhere,
        input_output_aliases={1: 0},
        scratch_shapes=[pltpu.SemaphoreType.DMA((got.shape[0],))],
        compiler_params=params(),
        cost_estimate=pl.CostEstimate(flops=0, bytes_accessed=4 * got.size, transcendentals=0),
    )(got, into)


def body(copies, devices, acts, grad_out, low_acts, up_weight, block_adapter, block_fill, owner_slot):
    own_blocks = block_fill.shape[0]
    blocks, adapters = block_adapter.shape[0], owner_slot.shape[0]
    own_slots, rank, out_width = up_weight.shape
    model_width = acts.shape[1]
    half_devices = devices // 2
    half_blocks, half_slots = blocks // 2, adapters // 2
    groups = [list(range(half_devices)), list(range(half_devices, devices))]
    across = [(i, (i + half_devices) % devices) for i in range(devices)]
    half = lax.axis_index("dp") // half_devices

    def within(x):
        return lax.all_to_all(x, "dp", 0, 0, axis_index_groups=groups, tiled=True)

    def relative(x, k):
        return lax.ppermute(x, "dp", [(i, i ^ k) for i in range(devices)]) if k else x

    ids = jnp.arange(adapters, dtype=jnp.int32)
    slot_of = jnp.sum(
        jnp.where(block_adapter[:, None] == ids[None, :], owner_slot[None, :], 0), axis=1
    )

    place_in_half = lax.axis_index("dp") % half_devices
    by_permutes = half_devices <= 8 and out_width // half_devices % 128 == 0
    up_held = up_products(block_fill, low_acts.T, grad_out, half_devices)
    if by_permutes:
        up_pieces = [
            lax.dynamic_index_in_dim(up_held, place_in_half ^ k, 0, False)
            for k in range(half_devices)
        ]
        up_pieces = [relative(x, k) for k, x in enumerate(up_pieces)]
    else:
        up_pieces = [within(up_held).reshape(half_blocks, rank, -1)]

    lane_groups = min(devices // 4, out_width // 128)
    row_groups = devices // lane_groups
    rows, lanes = rank // row_groups, out_width // lane_groups
    pieces = up_weight.reshape(own_slots, row_groups, rows, lane_groups, lanes)
    pieces = pieces.transpose(1, 3, 0, 2, 4).reshape(devices, own_slots, rows, lanes)
    part = lax.all_to_all(pieces, "dp", 0, 0, tiled=True).reshape(adapters, rows, lanes)
    picked = pick(slot_of, part).reshape(devices, own_blocks, rows, lanes)
    weights = lax.all_to_all(picked, "dp", 0, 0, tiled=True)

    mine = lax.dynamic_slice_in_dim(slot_of, half * half_blocks, half_blocks)
    spots = jnp.arange(half_blocks, dtype=jnp.int32)
    before = (mine[None, :] < mine[:, None]) | (
        (mine[None, :] == mine[:, None]) & (spots[None, :] < spots[:, None])
    )
    spot_of = jnp.sum(before.astype(jnp.int32), axis=1)
    order = jnp.sum(jnp.where(spot_of[None, :] == spots[:, None], spots[None, :], 0), axis=1)
    start = jnp.sum((mine[None, :] < ids[:, None]).astype(jnp.int32), axis=1)
    count = jnp.sum((mine[None, :] == ids[:, None]).astype(jnp.int32), axis=1)
    by_half = slot_of.reshape(2, half_blocks)
    has = jnp.any(by_half[:, :, None] == ids[None, None, :], axis=1)
    crosses = has & ((ids[None, :] // half_slots) != jnp.arange(2, dtype=jnp.int32)[:, None])
    earlier = (ids[None, :] < ids[:, None])[None, :, :]
    place_of = jnp.sum((crosses[:, None, :] & earlier).astype(jnp.int32), axis=2)
    used = jnp.any(has, axis=0).reshape(-1, own_slots)
    slot_ids = jnp.arange(own_slots, dtype=jnp.int32)
    rank_of = jnp.sum(
        (used[:, None, :] & (slot_ids[None, :] < slot_ids[:, None])[None]).astype(jnp.int32), axis=2
    )
    mine_needed = jnp.stack(
        [
            jnp.max(jnp.sum(crosses.astype(jnp.int32), axis=1)),
            jnp.max(jnp.sum(used.astype(jnp.int32), axis=1)),
        ]
    ).reshape(1, 2)
    needed = mine_needed
    for k in range(1, copies):
        shift = [(i, (i + k) % copies) for i in range(copies)]
        needed = jnp.maximum(needed, lax.ppermute(mine_needed, "groups", shift))
    needed, most = needed[0, 0], needed[0, 1]

    my_cross = lax.dynamic_index_in_dim(crosses, half, 0, False)
    my_place = lax.dynamic_index_in_dim(place_of, half, 0, False)
    hot = my_cross[None, :] & (my_place[None, :] == spots[:, None])
    send_first = jnp.sum(jnp.where(hot, start[None, :], 0), axis=1)
    send_last = jnp.sum(jnp.where(hot, (start + count)[None, :], 0), axis=1)

    own = half * half_slots
    keep_first = lax.dynamic_slice_in_dim(start, own, half_slots)
    keep_last = keep_first + lax.dynamic_slice_in_dim(count, own, half_slots)
    got = lax.dynamic_index_in_dim(crosses, 1 - half, 0, False)
    got = lax.dynamic_slice_in_dim(got, own, half_slots).astype(jnp.int32)
    got_first = lax.dynamic_index_in_dim(place_of, 1 - half, 0, False)
    got_first = lax.dynamic_slice_in_dim(got_first, own, half_slots)
    keep_table = jnp.concatenate([order, keep_first, keep_last, got_first, got_first + got])

    keep = jnp.stack([keep_first, keep_last, got_first, got_first + got])
    keep = keep.reshape(4, half_devices, 1, own_slots)
    half_used = lax.dynamic_slice_in_dim(used, half * half_devices, half_devices)
    half_rank = lax.dynamic_slice_in_dim(rank_of, half * half_devices, half_devices)
    chosen = half_used[:, None, :] & (half_rank[:, None, :] == slot_ids[None, :, None])
    packed = jnp.sum(jnp.where(chosen[None], keep, 0), axis=3)
    mine_at = lax.axis_index("dp")
    landing = jnp.where(
        lax.dynamic_index_in_dim(used, mine_at, 0, False),
        lax.dynamic_index_in_dim(rank_of, mine_at, 0, False),
        -1,
    )
    up_order = order
    if by_permutes:
        source, spot = order // own_blocks, order % own_blocks
        up_order = (source ^ place_in_half) * own_blocks + spot
    orders = jnp.concatenate([order, up_order])

    low_t = rank_cotangent(block_fill, weights, grad_out, lane_groups, rank, up_pieces)
    up_held = jnp.concatenate(up_pieces)
    first = within(products(low_t, acts, half_devices, 0))
    first = first.reshape(half_blocks, rank, -1)
    second = products(low_t, acts, half_devices, 1)
    width = second.shape[3]

    def rest(
        capacity, slots, first, up_held, second, orders, send_first, send_last, keep_table, packed,
        landing
    ):
        if slots < own_slots:
            ends = packed[:, :, :slots].reshape(-1)
        else:
            ends, landing = keep_table[half_blocks:], None
        keep_a_table = jnp.concatenate([orders, ends])
        keep_b_table = jnp.concatenate([orders[:half_blocks], ends])
        targets = half_devices * slots
        ends = jnp.concatenate([send_first[:capacity], send_last[:capacity]])
        send_a_table = jnp.concatenate([orders, ends])
        send_b_table = jnp.concatenate([orders[:half_blocks], ends])
        second = within(second).reshape(half_blocks, rank, -1)
        both = [first, up_held]
        (sent_a,) = slot_sums(send_a_table, both, capacity, SMALL)
        came_a = lax.ppermute(sent_a, "dp", across)
        (sent_b,) = slot_sums(send_b_table, [second], capacity, SMALL)
        came_a, sent_b = lax.optimization_barrier((came_a, sent_b))
        came_b = lax.ppermute(sent_b, "dp", across)
        (kept_a,) = slot_sums(
            keep_a_table, both, targets, SMALL, came_a, 1, (), GROUPS if by_permutes else 0
        )
        done_a = within(kept_a.reshape(half_devices, slots, rank, -1))
        up_width = out_width // half_devices
        if up_width % 128:
            up = done_a[:, :, :, width:].transpose(1, 2, 0, 3).reshape(own_slots, rank, out_width)
        else:
            up = place(done_a, landing, own_slots, up_width, width // up_width, out_width, 0)
        down = place(done_a, landing, own_slots, width, 0, model_width, 0)
        (kept_b,) = slot_sums(keep_b_table, [second], targets, LARGE, came_b, 1, (), GROUPS)
        done_b = within(kept_b.reshape(half_devices, slots, rank, -1))
        if landing is None:
            return lay(done_b, half_devices, down), up
        return place(done_b, landing, own_slots, width, 0, model_width, 1, down), up

    limit = min(half_blocks, half_slots)
    capacities = sorted({-(-limit * k // 24) for k in (9, 10, 11, 13, 24)})
    index = sum((needed > c).astype(jnp.int32) for c in capacities[:-1])
    sizes = [own_slots]
    if own_slots > 1 and out_width // half_devices % 128 == 0:
        sizes = [own_slots - 1, own_slots]
        index = 2 * index + (most >= own_slots).astype(jnp.int32)
    return lax.switch(
        index,
        [functools.partial(rest, c, n) for c in capacities for n in sizes],
        first, up_held, second, orders, send_first, send_last, keep_table, packed, landing,
    )


def solution(mesh):
    placed = (
        P(("groups", "dp"), None),
        P(("groups", "dp"), None),
        P(("groups", "dp"), None),
        P("dp", None, None),
        P("groups"),
        P(("groups", "dp")),
        P(),
    )
    return jax.shard_map(
        functools.partial(body, mesh.shape["groups"], mesh.shape["dp"]),
        mesh=mesh,
        in_specs=placed,
        out_specs=(P(("groups", "dp"), None, None), P(("groups", "dp"), None, None)),
        check_vma=False,
    )
```

profile of v0, /device:TPU:0, one launch (start us, length us, event | category | flops | bytes accessed | tf_op | source)
XLA Modules:
  0.0 197.3 jit_solution(16686782053018935155)
XLA Ops:
  3.1 7.4 %all-to-all-start.30 = ((bf16[16,4,16,256]{3,2,1,0:T(8,128)(2,1)}), bf16[16,4,16,256]{3,2,1,0:T(8,128)(2,1)S(1)}, u32[]{:S(2)}, u32[]{:S(2)}) async-start(bf16[16,4,16,256]{3,2,1,0:T(8,128)(2,1)} %bitcast.45), calls=%async_computation.30 | async-start | bytes 1048576 | tf_op jit(solution)/shard_map/all_to_all | solution.py:313
  11.4 2.6 %collective-permute-start.27 = (bf16[3,64,128]{2,1,0:T(8,128)(2,1)S(1)}, bf16[3,64,128]{2,1,0:T(8,128)(2,1)S(1)}, u32[]{:S(2)}, u32[]{:S(2)}) collective-permute-start(bf16[3,64,128]{2,1,0:T(8,128)(2,1)S(1)} %get-tuple-element.945), channel_id=1, source_target_pairs={{0,7},{1,6},{2,5},{3,4},{4,3},{5,2},{6,1},{7,0},{8,15},{9,14},{10,... | collective-permute-start | bytes 147464 | tf_op jit(solution)/shard_map/ppermute | solution.py:289
  18.2 7.1 %all-to-all-done.30 = bf16[16,4,16,256]{3,2,1,0:T(8,128)(2,1)S(1)} async-done(((bf16[16,4,16,256]{3,2,1,0:T(8,128)(2,1)}), bf16[16,4,16,256]{3,2,1,0:T(8,128)(2,1)S(1)}, u32[]{:S(2)}, u32[]{:S(2)}) %all-to-all-start.30) | async-done | bytes 524320 | tf_op jit(solution)/shard_map/all_to_all | solution.py:313
  26.9 3.9 %all-to-all-start.31 = ((bf16[16,3,16,256]{3,2,1,0:T(8,128)(2,1)}), bf16[16,3,16,256]{3,2,1,0:T(8,128)(2,1)S(1)}, u32[]{:S(2)}, u32[]{:S(2)}) async-start(bf16[16,3,16,256]{3,2,1,0:T(8,128)(2,1)} %bitcast.47), calls=%async_computation.31 | async-start | bytes 786432 | tf_op jit(solution)/shard_map/all_to_all | solution.py:315
  37.5 5.5 %all-to-all-done.31.parts_ref = bf16[16,3,16,256]{3,2,1,0:T(8,128)(2,1)S(1)} async-done(((bf16[16,3,16,256]{3,2,1,0:T(8,128)(2,1)}), bf16[16,3,16,256]{3,2,1,0:T(8,128)(2,1)S(1)}, u32[]{:S(2)}, u32[]{:S(2)}) %all-to-all-start.31) | async-done | bytes 393248 | tf_op jit(solution)/shard_map/all_to_all | solution.py:315
  43.9 3.1 %shard_map.110 = bf16[8,3,64,512]{3,2,1,0:T(8,128)(2,1)} custom-call(bf16[3,64,128]{2,1,0:T(8,128)(2,1)S(1)} %shard_map.108.low_ref, bf16[384,8192]{1,0:T(8,128)(2,1)} %acts_ref.3), custom_call_target="tpu_custom_call" | custom-call | flops 201326592 | bytes 4718592 | tf_op jit(solution)/shard_map/pallas_call | solution.py:119
  47.1 4.3 %all-to-all-start.32 = ((bf16[8,3,64,512]{3,2,1,0:T(8,128)(2,1)}), bf16[8,3,64,512]{3,2,1,0:T(8,128)(2,1)}, u32[]{:S(2)}, u32[]{:S(2)}) async-start(bf16[8,3,64,512]{3,2,1,0:T(8,128)(2,1)} %shard_map.110), calls=%async_computation.32 | async-start | bytes 3145728 | tf_op jit(solution)/shard_map/all_to_all | solution.py:286
  58.7 3.2 %shard_map.109 = bf16[8,3,64,512]{3,2,1,0:T(8,128)(2,1)} custom-call(bf16[3,64,128]{2,1,0:T(8,128)(2,1)S(1)} %shard_map.108.low_ref, bf16[384,8192]{1,0:T(8,128)(2,1)} %acts_ref.3), custom_call_target="tpu_custom_call" | custom-call | flops 201326592 | bytes 4718592 | tf_op jit(solution)/shard_map/pallas_call | solution.py:119
  61.9 9.6 %all-to-all-done.32 = bf16[8,3,64,512]{3,2,1,0:T(8,128)(2,1)} async-done(((bf16[8,3,64,512]{3,2,1,0:T(8,128)(2,1)}), bf16[8,3,64,512]{3,2,1,0:T(8,128)(2,1)}, u32[]{:S(2)}, u32[]{:S(2)}) %all-to-all-start.32) | async-done | bytes 1572896 | tf_op jit(solution)/shard_map/all_to_all | solution.py:286
  72.0 125.3 %conditional.1 = (bf16[4,64,8192]{2,1,0:T(8,128)(2,1)}, bf16[4,64,1024]{2,1,0:T(8,128)(2,1)}) conditional(s32[]{:T(128)} %bitcast.43, (s32[]{:T(128)}, pred[]{:T(512)}, pred[16,4]{1,0:T(8,128)(4,1)S(1)}, s32[16,4,4]{0,2,1:T(4,128)S(1)}, s32[]{:T(128)}, /*index=5*/s32[1,8,4,4]{1,3,2,0:T(4,128)S(1)}, ...), branch_computations={%region_14.17_spmd, %region_17.18_spmd, %region_18.21_spmd, %regio... | conditional | flops 274881052672 | bytes 274941345792 | solution.py:432
  72.0 3.6 %all-to-all-start.21 = ((bf16[8,3,64,512]{3,2,1,0:T(8,128)(2,1)}), bf16[8,3,64,512]{3,2,1,0:T(8,128)(2,1)S(1)}, u32[]{:S(2)}, u32[]{:S(2)}) async-start(bf16[8,3,64,512]{3,2,1,0:T(8,128)(2,1)} %get-tuple-element.505), calls=%async_computation.21 | async-start | bytes 3145728 | tf_op jit(solution)/shard_map/cond/branch_4_fun/all_to_all | solution.py:286
  75.7 2.1 %branch_4_fun.7 = bf16[11,64,640]{2,1,0:T(8,128)(2,1)S(1)} custom-call(s32[70]{0:T(128)S(1)} %pad_add_fusion.30.table_ref, bf16[24,64,512]{2,1,0:T(8,128)(2,1)} %get-tuple-element.509.refs_0_, bf16[24,64,128]{2,1,0:T(8,128)(2,1)S(1)} %get-tuple-element.510.refs_1_), custom_call_target="tpu_custom_call" | custom-call | flops 1048576 | bytes 1048576 | tf_op jit(solution)/shard_map/cond/branch_4_fun/pallas_call | solution.py:193
  80.3 30.4 %all-to-all-done.21 = bf16[8,3,64,512]{3,2,1,0:T(8,128)(2,1)S(1)} async-done(((bf16[8,3,64,512]{3,2,1,0:T(8,128)(2,1)}), bf16[8,3,64,512]{3,2,1,0:T(8,128)(2,1)S(1)}, u32[]{:S(2)}, u32[]{:S(2)}) %all-to-all-start.21) | async-done | bytes 1572896 | tf_op jit(solution)/shard_map/cond/branch_4_fun/all_to_all | solution.py:286
  112.6 7.9 %collective-permute-done.14.refs_2_ = bf16[11,64,640]{2,1,0:T(8,128)(2,1)S(1)} collective-permute-done((bf16[11,64,640]{2,1,0:T(8,128)(2,1)S(1)}, bf16[11,64,640]{2,1,0:T(8,128)(2,1)S(1)}, u32[]{:S(2)}, u32[]{:S(2)}) %collective-permute-start.14) | collective-permute-done | bytes 901152 | tf_op jit(solution)/shard_map/cond/branch_4_fun/ppermute | solution.py:405
  121.3 3.6 %branch_4_fun.10 = bf16[24,64,640]{2,1,0:T(8,128)(2,1)} custom-call(s32[144]{0:T(256)S(1)} %pad_add_fusion.28.table_ref, bf16[24,64,512]{2,1,0:T(8,128)(2,1)} %get-tuple-element.509.refs_0_, bf16[24,64,128]{2,1,0:T(8,128)(2,1)} %copy-done.16, bf16[11,64,640]{2,1,0:T(8,128)(2,1)S(1)} %collective-permute-done.14.refs_2_), custom_call_target="tpu_custom_call" | custom-call | flops 1048576 | bytes 1048576 | tf_op jit(solution)/shard_map/cond/branch_4_fun/pallas_call | solution.py:193
  125.0 5.4 %all-to-all-start.23 = ((bf16[8,3,64,640]{3,2,1,0:T(8,128)(2,1)}), bf16[8,3,64,640]{3,2,1,0:T(8,128)(2,1)}, u32[]{:S(2)}, u32[]{:S(2)}) async-start(bf16[8,3,64,640]{3,2,1,0:T(8,128)(2,1)} %bitcast.20), calls=%async_computation.23 | async-start | bytes 3932160 | tf_op jit(solution)/shard_map/cond/branch_4_fun/all_to_all | solution.py:286
  130.4 24.1 %collective-permute-done.15.refs_1_ = bf16[11,64,512]{2,1,0:T(8,128)(2,1)S(1)} collective-permute-done((bf16[11,64,512]{2,1,0:T(8,128)(2,1)}, bf16[11,64,512]{2,1,0:T(8,128)(2,1)S(1)}, u32[]{:S(2)}, u32[]{:S(2)}) %collective-permute-start.15) | collective-permute-done | bytes 720928 | tf_op jit(solution)/shard_map/cond/branch_4_fun/ppermute | solution.py:408
  154.5 2.3 %branch_4_fun.9 = bf16[24,64,512]{2,1,0:T(8,128)(2,1)} custom-call(s32[120]{0:T(128)S(1)} %pad_add_fusion.29.table_ref, bf16[24,64,512]{2,1,0:T(8,128)(2,1)S(1)} %bitcast.109, bf16[11,64,512]{2,1,0:T(8,128)(2,1)S(1)} %collective-permute-done.15.refs_1_), custom_call_target="tpu_custom_call" | custom-call | flops 274877906944 | bytes 274877906944 | tf_op jit(solution)/shard_map/cond/branch_4_fun/pallas_call | solution.py:193
  156.8 13.3 %all-to-all-done.23.refs_1_ = bf16[8,3,64,640]{3,2,1,0:T(8,128)(2,1)} async-done(((bf16[8,3,64,640]{3,2,1,0:T(8,128)(2,1)}), bf16[8,3,64,640]{3,2,1,0:T(8,128)(2,1)}, u32[]{:S(2)}, u32[]{:S(2)}) %all-to-all-start.23) | async-done | bytes 1966112 | tf_op jit(solution)/shard_map/cond/branch_4_fun/all_to_all | solution.py:286
  170.1 3.6 %all-to-all-start.22 = ((bf16[8,3,64,512]{3,2,1,0:T(8,128)(2,1)}), bf16[8,3,64,512]{3,2,1,0:T(8,128)(2,1)S(1)}, u32[]{:S(2)}, u32[]{:S(2)}) async-start(bf16[8,3,64,512]{3,2,1,0:T(8,128)(2,1)} %bitcast.19), calls=%async_computation.22 | async-start | bytes 3145728 | tf_op jit(solution)/shard_map/cond/branch_4_fun/all_to_all | solution.py:286
  173.9 4.7 %branch_4_fun.13 = bf16[4,64,1024]{2,1,0:T(8,128)(2,1)} custom-call(s32[4]{0:T(128)S(1)} %select_reduce_fusion.5.refs_0_, bf16[8,3,64,640]{3,2,1,0:T(8,128)(2,1)} %all-to-all-done.23.refs_1_), custom_call_target="tpu_custom_call" | custom-call | bytes 1048576 | tf_op jit(solution)/shard_map/cond/branch_4_fun/pallas_call | solution.py:232
  178.6 5.7 %branch_4_fun.11.refs_2_ = bf16[4,64,8192]{2,1,0:T(8,128)(2,1)} custom-call(s32[4]{0:T(128)S(1)} %select_reduce_fusion.5.refs_0_, bf16[8,3,64,640]{3,2,1,0:T(8,128)(2,1)} %all-to-all-done.23.refs_1_), custom_call_target="tpu_custom_call" | custom-call | bytes 4194304 | tf_op jit(solution)/shard_map/cond/branch_4_fun/pallas_call | solution.py:232
  184.2 9.4 %all-to-all-done.22.refs_1_ = bf16[8,3,64,512]{3,2,1,0:T(8,128)(2,1)S(1)} async-done(((bf16[8,3,64,512]{3,2,1,0:T(8,128)(2,1)}), bf16[8,3,64,512]{3,2,1,0:T(8,128)(2,1)S(1)}, u32[]{:S(2)}, u32[]{:S(2)}) %all-to-all-start.22) | async-done | bytes 1572896 | tf_op jit(solution)/shard_map/cond/branch_4_fun/all_to_all | solution.py:286
  193.7 3.6 %branch_4_fun.12 = bf16[4,64,8192]{2,1,0:T(8,128)(2,1)} custom-call(s32[4]{0:T(128)S(1)} %select_reduce_fusion.5.refs_0_, bf16[8,3,64,512]{3,2,1,0:T(8,128)(2,1)S(1)} %all-to-all-done.22.refs_1_, bf16[4,64,8192]{2,1,0:T(8,128)(2,1)} %branch_4_fun.11.refs_2_), custom_call_target="tpu_custom_call", output_to_operand_aliasing={{}: (2, {})} | custom-call | bytes 4194304 | tf_op jit(solution)/shard_map/cond/branch_4_fun/pallas_call | solution.py:232
  (109 shorter events, 26.7 us)
Async XLA Ops:
  0.6 9.9 %copy-start.7 = (s32[3]{0:T(128)S(1)}, s32[3]{0:T(128)}, u32[]{:S(2)}) copy-start(s32[3]{0:T(128)} %fill_ref.3) | copy-start | bytes 40
  0.6 9.9 %copy-start = (bf16[384,1024]{1,0:T(8,128)(2,1)S(1)}, bf16[384,1024]{1,0:T(8,128)(2,1)}, u32[]{:S(2)}) copy-start(bf16[384,1024]{1,0:T(8,128)(2,1)} %grad_ref.3) | copy-start | bytes 2359300
  0.7 9.9 %copy-start.6 = (bf16[384,64]{0,1:T(8,128)(2,1)S(1)}, bf16[384,64]{0,1:T(8,128)(2,1)}, u32[]{:S(2)}) copy-start(bf16[384,64]{0,1:T(8,128)(2,1)} %param.19) | copy-start | bytes 147460
  2.2 15.3 %copy-start.80 = (s32[64]{0:T(128)S(1)}, s32[64]{0:T(128)}, u32[]{:S(2)}) copy-start(s32[64]{0:T(128)} %param.23) | copy-start | bytes 772
  2.2 15.3 %copy-start.81 = (s32[48]{0:T(128)S(1)}, s32[48]{0:T(128)}, u32[]{:S(2)}) copy-start(s32[48]{0:T(128)} %param.21) | copy-start | bytes 580
  3.1 22.2 %all-to-all-start.30 = ((bf16[16,4,16,256]{3,2,1,0:T(8,128)(2,1)}), bf16[16,4,16,256]{3,2,1,0:T(8,128)(2,1)S(1)}, u32[]{:S(2)}, u32[]{:S(2)}) async-start(bf16[16,4,16,256]{3,2,1,0:T(8,128)(2,1)} %bitcast.45), calls=%async_computation.30 | async-start | bytes 1048576 | tf_op jit(solution)/shard_map/all_to_all | solution.py:313
  11.4 21.3 %collective-permute-start.27 = (bf16[3,64,128]{2,1,0:T(8,128)(2,1)S(1)}, bf16[3,64,128]{2,1,0:T(8,128)(2,1)S(1)}, u32[]{:S(2)}, u32[]{:S(2)}) collective-permute-start(bf16[3,64,128]{2,1,0:T(8,128)(2,1)S(1)} %get-tuple-element.945), channel_id=1, source_target_pairs={{0,7},{1,6},{2,5},{3,4},{4,3},{5,2},{6,1},{7,0},{8,15},{9,14},{10,... | collective-permute-start | bytes 147464 | tf_op jit(solution)/shard_map/ppermute | solution.py:289
  14.0 20.6 %collective-permute-start.26 = (bf16[3,64,128]{2,1,0:T(8,128)(2,1)S(1)}, bf16[3,64,128]{2,1,0:T(8,128)(2,1)S(1)}, u32[]{:S(2)}, u32[]{:S(2)}) collective-permute-start(bf16[3,64,128]{2,1,0:T(8,128)(2,1)S(1)} %get-tuple-element.946), channel_id=1, source_target_pairs={{0,6},{1,7},{2,4},{3,5},{4,2},{5,3},{6,0},{7,1},{8,14},{9,15},{10,... | collective-permute-start | bytes 147464 | tf_op jit(solution)/shard_map/ppermute | solution.py:289
  14.4 21.6 %collective-permute-start.25 = (bf16[3,64,128]{2,1,0:T(8,128)(2,1)S(1)}, bf16[3,64,128]{2,1,0:T(8,128)(2,1)S(1)}, u32[]{:S(2)}, u32[]{:S(2)}) collective-permute-start(bf16[3,64,128]{2,1,0:T(8,128)(2,1)S(1)} %get-tuple-element.947), channel_id=1, source_target_pairs={{0,5},{1,4},{2,7},{3,6},{4,1},{5,0},{6,3},{7,2},{8,13},{9,12},{10,... | collective-permute-start | bytes 147464 | tf_op jit(solution)/shard_map/ppermute | solution.py:289
  15.7 21.7 %collective-permute-start.24 = (bf16[3,64,128]{2,1,0:T(8,128)(2,1)S(1)}, bf16[3,64,128]{2,1,0:T(8,128)(2,1)S(1)}, u32[]{:S(2)}, u32[]{:S(2)}) collective-permute-start(bf16[3,64,128]{2,1,0:T(8,128)(2,1)S(1)} %get-tuple-element.948), channel_id=1, source_target_pairs={{0,4},{1,5},{2,6},{3,7},{4,0},{5,1},{6,2},{7,3},{8,12},{9,13},{10,... | collective-permute-start | bytes 147464 | tf_op jit(solution)/shard_map/ppermute | solution.py:289
  16.1 21.3 %collective-permute-start.23 = (bf16[3,64,128]{2,1,0:T(8,128)(2,1)S(1)}, bf16[3,64,128]{2,1,0:T(8,128)(2,1)S(1)}, u32[]{:S(2)}, u32[]{:S(2)}) collective-permute-start(bf16[3,64,128]{2,1,0:T(8,128)(2,1)S(1)} %get-tuple-element.949), channel_id=1, source_target_pairs={{0,3},{1,2},{2,1},{3,0},{4,7},{5,6},{6,5},{7,4},{8,11},{9,10},{10,... | collective-permute-start | bytes 147464 | tf_op jit(solution)/shard_map/ppermute | solution.py:289
  26.9 16.1 %all-to-all-start.31 = ((bf16[16,3,16,256]{3,2,1,0:T(8,128)(2,1)}), bf16[16,3,16,256]{3,2,1,0:T(8,128)(2,1)S(1)}, u32[]{:S(2)}, u32[]{:S(2)}) async-start(bf16[16,3,16,256]{3,2,1,0:T(8,128)(2,1)} %bitcast.47), calls=%async_computation.31 | async-start | bytes 786432 | tf_op jit(solution)/shard_map/all_to_all | solution.py:315
  32.7 4.7 %collective-permute-start.22 = (bf16[3,64,128]{2,1,0:T(8,128)(2,1)S(1)}, bf16[3,64,128]{2,1,0:T(8,128)(2,1)S(1)}, u32[]{:S(2)}, u32[]{:S(2)}) collective-permute-start(bf16[3,64,128]{2,1,0:T(8,128)(2,1)S(1)} %get-tuple-element.950), channel_id=1, source_target_pairs={{0,2},{1,3},{2,0},{3,1},{4,6},{5,7},{6,4},{7,5},{8,10},{9,11},{10,... | collective-permute-start | bytes 147464 | tf_op jit(solution)/shard_map/ppermute | solution.py:289
  34.6 2.8 %collective-permute-start.21 = (bf16[3,64,128]{2,1,0:T(8,128)(2,1)S(1)}, bf16[3,64,128]{2,1,0:T(8,128)(2,1)S(1)}, u32[]{:S(2)}, u32[]{:S(2)}) collective-permute-start(bf16[3,64,128]{2,1,0:T(8,128)(2,1)S(1)} %get-tuple-element.951), channel_id=1, source_target_pairs={{0,1},{1,0},{2,3},{3,2},{4,5},{5,4},{6,7},{7,6},{8,9},{9,8},{10,11... | collective-permute-start | bytes 147464 | tf_op jit(solution)/shard_map/ppermute | solution.py:289
  35.9 17.7 %collective-permute-start.20 = (s32[1,2]{1,0:T(1,128)S(1)}, s32[1,2]{1,0:T(1,128)S(1)}, u32[]{:S(2)}, u32[]{:S(2)}) collective-permute-start(s32[1,2]{1,0:T(1,128)S(1)} %add_bitcast_fusion), channel_id=1, source_target_pairs={{0,16},{16,0},{1,17},{17,1},{2,18},{18,2},{3,19},{19,3},{4,20},{20... | collective-permute-start | bytes 32 | tf_op jit(solution)/shard_map/ppermute | solution.py:345
  47.1 24.4 %all-to-all-start.32 = ((bf16[8,3,64,512]{3,2,1,0:T(8,128)(2,1)}), bf16[8,3,64,512]{3,2,1,0:T(8,128)(2,1)}, u32[]{:S(2)}, u32[]{:S(2)}) async-start(bf16[8,3,64,512]{3,2,1,0:T(8,128)(2,1)} %shard_map.110), calls=%async_computation.32 | async-start | bytes 3145728 | tf_op jit(solution)/shard_map/all_to_all | solution.py:286
  72.0 38.6 %all-to-all-start.21 = ((bf16[8,3,64,512]{3,2,1,0:T(8,128)(2,1)}), bf16[8,3,64,512]{3,2,1,0:T(8,128)(2,1)S(1)}, u32[]{:S(2)}, u32[]{:S(2)}) async-start(bf16[8,3,64,512]{3,2,1,0:T(8,128)(2,1)} %get-tuple-element.505), calls=%async_computation.21 | async-start | bytes 3145728 | tf_op jit(solution)/shard_map/cond/branch_4_fun/all_to_all | solution.py:286
  77.8 42.7 %collective-permute-start.14 = (bf16[11,64,640]{2,1,0:T(8,128)(2,1)S(1)}, bf16[11,64,640]{2,1,0:T(8,128)(2,1)S(1)}, u32[]{:S(2)}, u32[]{:S(2)}) collective-permute-start(bf16[11,64,640]{2,1,0:T(8,128)(2,1)S(1)} %branch_4_fun.7), channel_id=1, source_target_pairs={{0,8},{1,9},{2,10},{3,11},{4,12},{5,13},{6,14},{7,15},{8,0},{9,1},... | collective-permute-start | bytes 2703368 | tf_op jit(solution)/shard_map/cond/branch_4_fun/ppermute | solution.py:405
  80.2 40.6 %copy-start.73 = (pred[16,4]{0,1:T(4,128)(4,1)}, pred[16,4]{0,1:T(4,128)(4,1)S(1)}, u32[]{:S(2)}) copy-start(pred[16,4]{0,1:T(4,128)(4,1)S(1)} %copy.148) | copy-start | bytes 196 | tf_op jit(solution)/shard_map/cond
  120.5 34.0 %collective-permute-start.15 = (bf16[11,64,512]{2,1,0:T(8,128)(2,1)}, bf16[11,64,512]{2,1,0:T(8,128)(2,1)S(1)}, u32[]{:S(2)}, u32[]{:S(2)}) collective-permute-start(bf16[11,64,512]{2,1,0:T(8,128)(2,1)} %branch_4_fun.8), channel_id=1, source_target_pairs={{0,8},{1,9},{2,10},{3,11},{4,12},{5,13},{6,14},{7,15},{8,0},{9,1},... | collective-permute-start | bytes 2162696 | tf_op jit(solution)/shard_map/cond/branch_4_fun/ppermute | solution.py:408
  125.0 45.1 %all-to-all-start.23 = ((bf16[8,3,64,640]{3,2,1,0:T(8,128)(2,1)}), bf16[8,3,64,640]{3,2,1,0:T(8,128)(2,1)}, u32[]{:S(2)}, u32[]{:S(2)}) async-start(bf16[8,3,64,640]{3,2,1,0:T(8,128)(2,1)} %bitcast.20), calls=%async_computation.23 | async-start | bytes 3932160 | tf_op jit(solution)/shard_map/cond/branch_4_fun/all_to_all | solution.py:286
  156.7 17.0 %copy-start.68 = (s32[16,4]{0,1:T(4,128)S(1)}, s32[16,4]{0,1:T(4,128)}, u32[]{:S(2)}) copy-start(s32[16,4]{0,1:T(4,128)} %copy-done.67) | copy-start | bytes 772 | tf_op jit(solution)/shard_map/cond
  156.7 17.0 %copy-start.74 = (pred[16,4]{0,1:T(4,128)(4,1)S(1)}, pred[16,4]{0,1:T(4,128)(4,1)}, u32[]{:S(2)}) copy-start(pred[16,4]{0,1:T(4,128)(4,1)} %copy-done.73) | copy-start | bytes 196 | tf_op jit(solution)/shard_map/cond
  170.1 23.6 %all-to-all-start.22 = ((bf16[8,3,64,512]{3,2,1,0:T(8,128)(2,1)}), bf16[8,3,64,512]{3,2,1,0:T(8,128)(2,1)S(1)}, u32[]{:S(2)}, u32[]{:S(2)}) async-start(bf16[8,3,64,512]{3,2,1,0:T(8,128)(2,1)} %bitcast.19), calls=%async_computation.22 | async-start | bytes 3145728 | tf_op jit(solution)/shard_map/cond/branch_4_fun/all_to_all | solution.py:286
  (3 other events, 8.0 us)
where the time goes:
time: 199 us; the launch traced here: 197 us
  waiting for transfers between devices  107 us (54%)
  starting transfers between devices  39.2 us (20%)
  Pallas kernels  33.5 us (17%)
  other arithmetic  6.53 us (3%)
  local copies, waits for them, and re-layouts  6.4 us (3%)
  between operations  4.11 us (2%)
    all_to_all x4, waiting for transfers between devices, within(): return lax.all_to_all(x, 'dp', 0, 0, axis_index_groups=groups, tiled=True)  62.7 us
    ppermute x1, waiting for transfers between devices, rest(): came_b = lax.ppermute(sent_b, 'dp', across)  24.1 us
    all_to_all x4, starting transfers between devices, within(): return lax.all_to_all(x, 'dp', 0, 0, axis_index_groups=groups, tiled=True)  16.8 us
    pallas_call x3, Pallas kernels, place(): pl.pallas_call(place_all_kernel if landing is None else place_kernel, gri...  14 us
    pallas_call x4, Pallas kernels, slot_sums(): pl.pallas_call(functools.partial(sum_kernel, blocks, len(held), extra is...  9.93 us
    ppermute x7, starting transfers between devices, relative(): lax.ppermute(x, 'dp', [(i, i ^ k) for i in range(devices)])  8.02 us
    ppermute x1, waiting for transfers between devices, rest(): came_a = lax.ppermute(sent_a, 'dp', across)  7.93 us
    all_to_all x1, starting transfers between devices, body(): lax.all_to_all(pieces, 'dp', 0, 0, tiled=True)  7.39 us
  transfers between devices with their start and end apart: 16, of which 8 were waited for; matrix products, arithmetic and copies ran while one was open for 5% of the time, Pallas kernels for 15%

commit v1 on v0

--- a/solution.py
+++ b/solution.py
@@ -243,32 +243,65 @@
     )(*operands)
 
 
-def lay_kernel(first, got_ref, _, out_ref, sems):
-    parts, _, _, width = got_ref.shape
-    copies = [
-        pltpu.make_async_copy(
-            got_ref.at[p], out_ref.at[:, :, pl.ds((first + p) * width, width)], sems.at[p]
-        )
-        for p in range(parts)
-    ]
-    for copy in copies:
-        copy.start()
-    for copy in copies:
-        copy.wait()
-
-
-def lay(got, first, into):
+def lay_kernel(first, width, has_landing, *refs):
+    landing_ref, refs = (refs[0], refs[1:]) if has_landing else (None, refs)
+    got_ref, _, down_ref, up_ref, zero, sems = refs
+    parts, held, rank, whole = got_ref.shape
+    waits = []
+    if has_landing:
+        zero[...] = jnp.zeros_like(zero)
+    for p in range(parts):
+        for o, (out, low, high, at) in enumerate(
+            [(down_ref, 0, width, first + p), (up_ref, width, whole, p)]
+        ):
+            columns = pl.ds(at * (high - low), high - low)
+            if not has_landing:
+                copy = pltpu.make_async_copy(
+                    got_ref.at[p, :, :, low:high], out.at[:, :, columns], sems.at[o, p, 0]
+                )
+                copy.start()
+                waits.append(copy)
+                continue
+            for n in range(out.shape[0]):
+                to = out.at[n, :, columns]
+                sem = sems.at[o, p, n]
+                none = pltpu.make_async_copy(zero.at[:, : high - low], to, sem)
+
+                @pl.when(landing_ref[n] >= 0)
+                def _(p=p, n=n, to=to, sem=sem, low=low, high=high):
+                    spot = jnp.maximum(landing_ref[n], 0)
+                    pltpu.make_async_copy(got_ref.at[p, spot, :, low:high], to, sem).start()
+
+                @pl.when(landing_ref[n] < 0)
+                def _(none=none):
+                    none.start()
+
+                waits.append(none)
+    for wait in waits:
+        wait.wait()
+
+
+def lay(got, landing, first, width, into, out_width):
+    parts, _, rank, _ = got.shape
     anywhere = pl.BlockSpec(memory_space=pl.ANY)
-    return pl.pallas_call(
-        functools.partial(lay_kernel, first),
-        out_shape=jax.ShapeDtypeStruct(into.shape, BF16),
-        in_specs=[anywhere, anywhere],
-        out_specs=anywhere,
-        input_output_aliases={1: 0},
-        scratch_shapes=[pltpu.SemaphoreType.DMA((got.shape[0],))],
+    operands = ([] if landing is None else [landing]) + [got, into]
+    specs = [] if landing is None else [pl.BlockSpec(memory_space=pltpu.SMEM)]
+    return pl.pallas_call(
+        functools.partial(lay_kernel, first, width, landing is not None),
+        out_shape=[
+            jax.ShapeDtypeStruct(into.shape, BF16),
+            jax.ShapeDtypeStruct(into.shape[:2] + (out_width,), BF16),
+        ],
+        in_specs=specs + [anywhere, anywhere],
+        out_specs=[anywhere, anywhere],
+        input_output_aliases={len(operands) - 1: 0},
+        scratch_shapes=[
+            pltpu.VMEM((rank, width), BF16),
+            pltpu.SemaphoreType.DMA((2, parts, into.shape[0])),
+        ],
         compiler_params=params(),
         cost_estimate=pl.CostEstimate(flops=0, bytes_accessed=4 * got.size, transcendentals=0),
-    )(got, into)
+    )(*operands)
 
 
 def body(copies, devices, acts, grad_out, low_acts, up_weight, block_adapter, block_fill, owner_slot):
@@ -393,40 +426,34 @@
             ends = packed[:, :, :slots].reshape(-1)
         else:
             ends, landing = keep_table[half_blocks:], None
-        keep_a_table = jnp.concatenate([orders, ends])
-        keep_b_table = jnp.concatenate([orders[:half_blocks], ends])
+        keep_a_table = jnp.concatenate([orders[:half_blocks], ends])
+        keep_b_table = jnp.concatenate([orders, ends])
         targets = half_devices * slots
         ends = jnp.concatenate([send_first[:capacity], send_last[:capacity]])
-        send_a_table = jnp.concatenate([orders, ends])
-        send_b_table = jnp.concatenate([orders[:half_blocks], ends])
-        second = within(second).reshape(half_blocks, rank, -1)
-        both = [first, up_held]
-        (sent_a,) = slot_sums(send_a_table, both, capacity, SMALL)
+        send_a_table = jnp.concatenate([orders[:half_blocks], ends])
+        send_b_table = jnp.concatenate([orders, ends])
+        groups = GROUPS if by_permutes else 0
+        both = [within(second).reshape(half_blocks, rank, -1), up_held]
+        (sent_a,) = slot_sums(send_a_table, [first], capacity, SMALL)
         came_a = lax.ppermute(sent_a, "dp", across)
-        (sent_b,) = slot_sums(send_b_table, [second], capacity, SMALL)
+        (sent_b,) = slot_sums(send_b_table, both, capacity, SMALL)
         came_a, sent_b = lax.optimization_barrier((came_a, sent_b))
         came_b = lax.ppermute(sent_b, "dp", across)
-        (kept_a,) = slot_sums(
-            keep_a_table, both, targets, SMALL, came_a, 1, (), GROUPS if by_permutes else 0
-        )
+        (kept_a,) = slot_sums(keep_a_table, [first], targets, SMALL, came_a, 1, (), groups)
         done_a = within(kept_a.reshape(half_devices, slots, rank, -1))
-        up_width = out_width // half_devices
-        if up_width % 128:
-            up = done_a[:, :, :, width:].transpose(1, 2, 0, 3).reshape(own_slots, rank, out_width)
-        else:
-            up = place(done_a, landing, own_slots, up_width, width // up_width, out_width, 0)
         down = place(done_a, landing, own_slots, width, 0, model_width, 0)
-        (kept_b,) = slot_sums(keep_b_table, [second], targets, LARGE, came_b, 1, (), GROUPS)
+        (kept_b,) = slot_sums(keep_b_table, both, targets, LARGE, came_b, 1, (), groups)
         done_b = within(kept_b.reshape(half_devices, slots, rank, -1))
-        if landing is None:
-            return lay(done_b, half_devices, down), up
+        if by_permutes:
+            return tuple(lay(done_b, landing, half_devices, width, down, out_width))
+        up = done_b[:, :, :, width:].transpose(1, 2, 0, 3).reshape(own_slots, rank, out_width)
         return place(done_b, landing, own_slots, width, 0, model_width, 1, down), up
 
     limit = min(half_blocks, half_slots)
     capacities = sorted({-(-limit * k // 24) for k in (9, 10, 11, 13, 24)})
     index = sum((needed > c).astype(jnp.int32) for c in capacities[:-1])
     sizes = [own_slots]
-    if own_slots > 1 and out_width // half_devices % 128 == 0:
+    if own_slots > 1 and by_permutes:
         sizes = [own_slots - 1, own_slots]
         index = 2 * index + (most >= own_slots).astype(jnp.int32)
     return lax.switch(

time: 199 us -> 202 us (1.015)
  Pallas kernels: 33.5 us -> 27.2 us
  local copies, waits for them, and re-layouts: 6.4 us -> 11.4 us
  waiting for transfers between devices: 107 us -> 110 us
    pallas_call x3 -> x1, Pallas kernels: 14 us -> 5.64 us  [place(): pl.pallas_call(place_all_kernel if landing is None else place_kernel, gri...]
    ppermute x1, waiting for transfers between devices: 7.93 us -> 0.01 us  [rest(): came_a = lax.ppermute(sent_a, 'dp', across)]
    ppermute x1, waiting for transfers between devices: 24.1 us -> 30.6 us  [rest(): came_b = lax.ppermute(sent_b, 'dp', across)]
    all_to_all x4, waiting for transfers between devices: 62.7 us -> 67.7 us  [within(): return lax.all_to_all(x, 'dp', 0, 0, axis_index_groups=groups, tiled=True)]
    unnamed x20, local copies, waits for them, and re-layouts: 0.12 us -> 4.38 us
    pallas_call x0 -> x1, Pallas kernels: none -> 2.03 us  [lay(): pl.pallas_call(functools.partial(lay_kernel, first, width, landing is not...]
  transfers between devices with their start and end apart: 16 -> 16, of which waited for: 8 -> 7; matrix products, arithmetic and copies ran while one was open for 5% -> 7% of each run, Pallas kernels for 15% -> 13%
where the time goes in v1:
time: 202 us; the launch traced here: 199 us
  waiting for transfers between devices  110 us (54%)
  starting transfers between devices  38.2 us (19%)
  Pallas kernels  27.2 us (13%)
  local copies, waits for them, and re-layouts  11.4 us (6%)
  other arithmetic  6.63 us (3%)
  between operations  4.54 us (2%)
    all_to_all x4, waiting for transfers between devices, within(): return lax.all_to_all(x, 'dp', 0, 0, axis_index_groups=groups, tiled=True)  67.7 us
    ppermute x1, waiting for transfers between devices, rest(): came_b = lax.ppermute(sent_b, 'dp', across)  30.6 us
    all_to_all x4, starting transfers between devices, within(): return lax.all_to_all(x, 'dp', 0, 0, axis_index_groups=groups, tiled=True)  15.3 us
    pallas_call x4, Pallas kernels, slot_sums(): pl.pallas_call(functools.partial(sum_kernel, blocks, len(held), extra is...  9.95 us
    ppermute x7, starting transfers between devices, relative(): lax.ppermute(x, 'dp', [(i, i ^ k) for i in range(devices)])  8.02 us
    all_to_all x1, starting transfers between devices, body(): lax.all_to_all(pieces, 'dp', 0, 0, tiled=True)  7.39 us
    all_to_all x1, waiting for transfers between devices, body(): lax.all_to_all(pieces, 'dp', 0, 0, tiled=True)  7.11 us
    pallas_call x2, Pallas kernels, products(): pl.pallas_call(down_kernel, grid=(steps,), out_shape=jax.ShapeDtypeStruct...  6.28 us
  transfers between devices with their start and end apart: 16, of which 7 were waited for; matrix products, arithmetic and copies ran while one was open for 7% of the time, Pallas kernels for 13%

profile of v1, /device:TPU:0, one launch (start us, length us, event | category | flops | bytes accessed | tf_op | source)
XLA Modules:
  0.0 198.7 jit_solution(11198666196689841540)
XLA Ops:
  3.1 7.4 %all-to-all-start.30 = ((bf16[16,4,16,256]{3,2,1,0:T(8,128)(2,1)}), bf16[16,4,16,256]{3,2,1,0:T(8,128)(2,1)S(1)}, u32[]{:S(2)}, u32[]{:S(2)}) async-start(bf16[16,4,16,256]{3,2,1,0:T(8,128)(2,1)} %bitcast.45), calls=%async_computation.30 | async-start | bytes 1048576 | tf_op jit(solution)/shard_map/all_to_all | solution.py:346
  11.4 2.6 %collective-permute-start.27 = (bf16[3,64,128]{2,1,0:T(8,128)(2,1)S(1)}, bf16[3,64,128]{2,1,0:T(8,128)(2,1)S(1)}, u32[]{:S(2)}, u32[]{:S(2)}) collective-permute-start(bf16[3,64,128]{2,1,0:T(8,128)(2,1)S(1)} %get-tuple-element.965), channel_id=1, source_target_pairs={{0,7},{1,6},{2,5},{3,4},{4,3},{5,2},{6,1},{7,0},{8,15},{9,14},{10,... | collective-permute-start | bytes 147464 | tf_op jit(solution)/shard_map/ppermute | solution.py:322
  18.2 7.1 %all-to-all-done.30 = bf16[16,4,16,256]{3,2,1,0:T(8,128)(2,1)S(1)} async-done(((bf16[16,4,16,256]{3,2,1,0:T(8,128)(2,1)}), bf16[16,4,16,256]{3,2,1,0:T(8,128)(2,1)S(1)}, u32[]{:S(2)}, u32[]{:S(2)}) %all-to-all-start.30) | async-done | bytes 524320 | tf_op jit(solution)/shard_map/all_to_all | solution.py:346
  26.9 3.9 %all-to-all-start.31 = ((bf16[16,3,16,256]{3,2,1,0:T(8,128)(2,1)}), bf16[16,3,16,256]{3,2,1,0:T(8,128)(2,1)S(1)}, u32[]{:S(2)}, u32[]{:S(2)}) async-start(bf16[16,3,16,256]{3,2,1,0:T(8,128)(2,1)} %bitcast.47), calls=%async_computation.31 | async-start | bytes 786432 | tf_op jit(solution)/shard_map/all_to_all | solution.py:348
  33.4 1.9 collective-permute-start.22
  38.3 4.7 %all-to-all-done.31.parts_ref = bf16[16,3,16,256]{3,2,1,0:T(8,128)(2,1)S(1)} async-done(((bf16[16,3,16,256]{3,2,1,0:T(8,128)(2,1)}), bf16[16,3,16,256]{3,2,1,0:T(8,128)(2,1)S(1)}, u32[]{:S(2)}, u32[]{:S(2)}) %all-to-all-start.31) | async-done | bytes 393248 | tf_op jit(solution)/shard_map/all_to_all | solution.py:348
  43.9 3.1 %shard_map.110 = bf16[8,3,64,512]{3,2,1,0:T(8,128)(2,1)} custom-call(bf16[3,64,128]{2,1,0:T(8,128)(2,1)S(1)} %shard_map.108.low_ref, bf16[384,8192]{1,0:T(8,128)(2,1)} %acts_ref.3), custom_call_target="tpu_custom_call" | custom-call | flops 201326592 | bytes 4718592 | tf_op jit(solution)/shard_map/pallas_call | solution.py:119
  47.1 3.6 %all-to-all-start.32 = ((bf16[8,3,64,512]{3,2,1,0:T(8,128)(2,1)}), bf16[8,3,64,512]{3,2,1,0:T(8,128)(2,1)S(1)}, u32[]{:S(2)}, u32[]{:S(2)}) async-start(bf16[8,3,64,512]{3,2,1,0:T(8,128)(2,1)} %shard_map.110), calls=%async_computation.32 | async-start | bytes 3145728 | tf_op jit(solution)/shard_map/all_to_all | solution.py:319
  62.6 3.1 %shard_map.109 = bf16[8,3,64,512]{3,2,1,0:T(8,128)(2,1)} custom-call(bf16[3,64,128]{2,1,0:T(8,128)(2,1)S(1)} %shard_map.108.low_ref, bf16[384,8192]{1,0:T(8,128)(2,1)} %acts_ref.3), custom_call_target="tpu_custom_call" | custom-call | flops 201326592 | bytes 4718592 | tf_op jit(solution)/shard_map/pallas_call | solution.py:119
  65.7 4.9 %all-to-all-done.32 = bf16[8,3,64,512]{3,2,1,0:T(8,128)(2,1)S(1)} async-done(((bf16[8,3,64,512]{3,2,1,0:T(8,128)(2,1)}), bf16[8,3,64,512]{3,2,1,0:T(8,128)(2,1)S(1)}, u32[]{:S(2)}, u32[]{:S(2)}) %all-to-all-start.32) | async-done | bytes 1572896 | tf_op jit(solution)/shard_map/all_to_all | solution.py:319
  71.2 127.3 %conditional.1 = ((bf16[4,64,8192]{2,1,0:T(8,128)(2,1)}, bf16[4,64,1024]{2,1,0:T(8,128)(2,1)})) conditional(s32[]{:T(128)} %bitcast.43, (s32[]{:T(128)}, pred[]{:T(512)}, pred[16,4]{1,0:T(8,128)(4,1)S(1)}, s32[16,4,4]{0,2,1:T(4,128)S(1)}, s32[]{:T(128)}, /*index=5*/s32[1,8,4,4]{1,3,2,0:T(4,128)S(1)}, ...), branch_computations={%region_14.17_spmd, %region_17.18_spmd, %region_18.21_spmd, %regio... | conditional | flops 274881052672 | bytes 274946588672 | solution.py:459
  71.2 3.6 %all-to-all-start.3 = ((bf16[8,3,64,512]{3,2,1,0:T(8,128)(2,1)}), bf16[8,3,64,512]{3,2,1,0:T(8,128)(2,1)S(1)}, u32[]{:S(2)}, u32[]{:S(2)}) async-start(bf16[8,3,64,512]{3,2,1,0:T(8,128)(2,1)} %get-tuple-element.489), calls=%async_computation.3 | async-start | bytes 3145728 | tf_op jit(solution)/shard_map/cond/branch_3_fun/all_to_all | solution.py:319
  74.9 1.7 branch_3_fun.6
  76.6 2.1 %collective-permute-start.2 = (bf16[10,64,512]{2,1,0:T(8,128)(2,1)}, bf16[10,64,512]{2,1,0:T(8,128)(2,1)S(1)}, u32[]{:S(2)}, u32[]{:S(2)}) collective-permute-start(bf16[10,64,512]{2,1,0:T(8,128)(2,1)} %branch_3_fun.6), channel_id=1, source_target_pairs={{0,8},{1,9},{2,10},{3,11},{4,12},{5,13},{6,14},{7,15},{8,0},{9,1},... | collective-permute-start | bytes 1966088 | tf_op jit(solution)/shard_map/cond/branch_3_fun/ppermute | solution.py:438
  78.7 30.2 %all-to-all-done.3 = bf16[8,3,64,512]{3,2,1,0:T(8,128)(2,1)S(1)} async-done(((bf16[8,3,64,512]{3,2,1,0:T(8,128)(2,1)}), bf16[8,3,64,512]{3,2,1,0:T(8,128)(2,1)S(1)}, u32[]{:S(2)}, u32[]{:S(2)}) %all-to-all-start.3) | async-done | bytes 1572896 | tf_op jit(solution)/shard_map/cond/branch_3_fun/all_to_all | solution.py:319
  110.7 2.7 %branch_3_fun.9 = bf16[32,64,512]{2,1,0:T(8,128)(2,1)} custom-call(s32[152]{0:T(256)S(1)} %pad_add_fusion.5.table_ref, bf16[24,64,512]{2,1,0:T(8,128)(2,1)S(1)} %copy-done.18, bf16[10,64,512]{2,1,0:T(8,128)(2,1)S(1)} %collective-permute-done.2.refs_1_), custom_call_target="tpu_custom_call" | custom-call | flops 1048576 | bytes 1048576 | tf_op jit(solution)/shard_map/cond/branch_3_fun/pallas_call | solution.py:193
  113.4 4.5 %all-to-all-start.5 = ((bf16[8,4,64,512]{3,2,1,0:T(8,128)(2,1)}), bf16[8,4,64,512]{3,2,1,0:T(8,128)(2,1)}, u32[]{:S(2)}, u32[]{:S(2)}) async-start(bf16[8,4,64,512]{3,2,1,0:T(8,128)(2,1)} %bitcast.15), calls=%async_computation.5 | async-start | bytes 4194304 | tf_op jit(solution)/shard_map/cond/branch_3_fun/all_to_all | solution.py:319
  117.9 30.6 %collective-permute-done.3.refs_2_ = bf16[10,64,640]{2,1,0:T(8,128)(2,1)} collective-permute-done((bf16[10,64,640]{2,1,0:T(8,128)(2,1)S(1)}, bf16[10,64,640]{2,1,0:T(8,128)(2,1)}, u32[]{:S(2)}, u32[]{:S(2)}) %collective-permute-start.3) | collective-permute-done | bytes 819232 | tf_op jit(solution)/shard_map/cond/branch_3_fun/ppermute | solution.py:441
  148.5 4.1 %branch_3_fun.8 = bf16[32,64,640]{2,1,0:T(8,128)(2,1)S(1)} custom-call(s32[176]{0:T(256)S(1)} %pad_add_fusion.4.table_ref, bf16[24,64,512]{2,1,0:T(8,128)(2,1)S(1)} %bitcast.115, bf16[24,64,128]{2,1,0:T(8,128)(2,1)S(1)} %copy-done.30, bf16[10,64,640]{2,1,0:T(8,128)(2,1)} %collective-permute-done.3.refs_2_), custom_call_target="tpu_custom_call" | custom-call | flops 274877906944 | bytes 274877906944 | tf_op jit(solution)/shard_map/cond/branch_3_fun/pallas_call | solution.py:193
  154.1 7.0 %all-to-all-done.5.got_ref = bf16[8,4,64,512]{3,2,1,0:T(8,128)(2,1)} async-done(((bf16[8,4,64,512]{3,2,1,0:T(8,128)(2,1)}), bf16[8,4,64,512]{3,2,1,0:T(8,128)(2,1)}, u32[]{:S(2)}, u32[]{:S(2)}) %all-to-all-start.5) | async-done | bytes 2097184 | tf_op jit(solution)/shard_map/cond/branch_3_fun/all_to_all | solution.py:319
  161.1 3.6 %all-to-all-start.4 = ((bf16[8,4,64,640]{3,2,1,0:T(8,128)(2,1)}), bf16[8,4,64,640]{3,2,1,0:T(8,128)(2,1)S(1)}, u32[]{:S(2)}, u32[]{:S(2)}) async-start(bf16[8,4,64,640]{3,2,1,0:T(8,128)(2,1)} %bitcast.125), calls=%async_computation.4 | async-start | bytes 5242880 | tf_op jit(solution)/shard_map/cond/branch_3_fun/all_to_all | solution.py:319
  164.7 5.6 %branch_3_fun.10.refs_1_ = bf16[4,64,8192]{2,1,0:T(8,128)(2,1)} custom-call(bf16[8,4,64,512]{3,2,1,0:T(8,128)(2,1)} %all-to-all-done.5.got_ref), custom_call_target="tpu_custom_call" | custom-call | bytes 4194304 | tf_op jit(solution)/shard_map/cond/branch_3_fun/pallas_call | solution.py:232
  170.3 25.6 %all-to-all-done.4.refs_0_ = bf16[8,4,64,640]{3,2,1,0:T(8,128)(2,1)S(1)} async-done(((bf16[8,4,64,640]{3,2,1,0:T(8,128)(2,1)}), bf16[8,4,64,640]{3,2,1,0:T(8,128)(2,1)S(1)}, u32[]{:S(2)}, u32[]{:S(2)}) %all-to-all-start.4) | async-done | bytes 2621472 | tf_op jit(solution)/shard_map/cond/branch_3_fun/all_to_all | solution.py:319
  195.9 2.0 %branch_3_fun.11 = (bf16[4,64,8192]{2,1,0:T(8,128)(2,1)}, bf16[4,64,1024]{2,1,0:T(8,128)(2,1)}) custom-call(bf16[8,4,64,640]{3,2,1,0:T(8,128)(2,1)S(1)} %all-to-all-done.4.refs_0_, bf16[4,64,8192]{2,1,0:T(8,128)(2,1)} %branch_3_fun.10.refs_1_), custom_call_target="tpu_custom_call", output_to_operand_aliasing={{0}: (1, {})} | custom-call | bytes 5242880 | tf_op jit(solution)/shard_map/cond/branch_3_fun/pallas_call | solution.py:289
  (95 shorter events, 28.0 us)
Async XLA Ops:
  0.6 9.9 %copy-start.12 = (s32[3]{0:T(128)S(1)}, s32[3]{0:T(128)}, u32[]{:S(2)}) copy-start(s32[3]{0:T(128)} %fill_ref.3) | copy-start | bytes 40
  0.6 9.9 %copy-start = (bf16[384,1024]{1,0:T(8,128)(2,1)S(1)}, bf16[384,1024]{1,0:T(8,128)(2,1)}, u32[]{:S(2)}) copy-start(bf16[384,1024]{1,0:T(8,128)(2,1)} %grad_ref.3) | copy-start | bytes 2359300
  0.7 9.9 %copy-start.11 = (bf16[384,64]{0,1:T(8,128)(2,1)S(1)}, bf16[384,64]{0,1:T(8,128)(2,1)}, u32[]{:S(2)}) copy-start(bf16[384,64]{0,1:T(8,128)(2,1)} %param.19) | copy-start | bytes 147460
  2.2 15.3 %copy-start.75 = (s32[64]{0:T(128)S(1)}, s32[64]{0:T(128)}, u32[]{:S(2)}) copy-start(s32[64]{0:T(128)} %param.23) | copy-start | bytes 772
  2.2 15.3 %copy-start.76 = (s32[48]{0:T(128)S(1)}, s32[48]{0:T(128)}, u32[]{:S(2)}) copy-start(s32[48]{0:T(128)} %param.21) | copy-start | bytes 580
  3.1 22.2 %all-to-all-start.30 = ((bf16[16,4,16,256]{3,2,1,0:T(8,128)(2,1)}), bf16[16,4,16,256]{3,2,1,0:T(8,128)(2,1)S(1)}, u32[]{:S(2)}, u32[]{:S(2)}) async-start(bf16[16,4,16,256]{3,2,1,0:T(8,128)(2,1)} %bitcast.45), calls=%async_computation.30 | async-start | bytes 1048576 | tf_op jit(solution)/shard_map/all_to_all | solution.py:346
  11.4 22.0 %collective-permute-start.27 = (bf16[3,64,128]{2,1,0:T(8,128)(2,1)S(1)}, bf16[3,64,128]{2,1,0:T(8,128)(2,1)S(1)}, u32[]{:S(2)}, u32[]{:S(2)}) collective-permute-start(bf16[3,64,128]{2,1,0:T(8,128)(2,1)S(1)} %get-tuple-element.965), channel_id=1, source_target_pairs={{0,7},{1,6},{2,5},{3,4},{4,3},{5,2},{6,1},{7,0},{8,15},{9,14},{10,... | collective-permute-start | bytes 147464 | tf_op jit(solution)/shard_map/ppermute | solution.py:322
  14.0 21.3 %collective-permute-start.26 = (bf16[3,64,128]{2,1,0:T(8,128)(2,1)S(1)}, bf16[3,64,128]{2,1,0:T(8,128)(2,1)S(1)}, u32[]{:S(2)}, u32[]{:S(2)}) collective-permute-start(bf16[3,64,128]{2,1,0:T(8,128)(2,1)S(1)} %get-tuple-element.966), channel_id=1, source_target_pairs={{0,6},{1,7},{2,4},{3,5},{4,2},{5,3},{6,0},{7,1},{8,14},{9,15},{10,... | collective-permute-start | bytes 147464 | tf_op jit(solution)/shard_map/ppermute | solution.py:322
  14.4 22.4 %collective-permute-start.25 = (bf16[3,64,128]{2,1,0:T(8,128)(2,1)S(1)}, bf16[3,64,128]{2,1,0:T(8,128)(2,1)S(1)}, u32[]{:S(2)}, u32[]{:S(2)}) collective-permute-start(bf16[3,64,128]{2,1,0:T(8,128)(2,1)S(1)} %get-tuple-element.967), channel_id=1, source_target_pairs={{0,5},{1,4},{2,7},{3,6},{4,1},{5,0},{6,3},{7,2},{8,13},{9,12},{10,... | collective-permute-start | bytes 147464 | tf_op jit(solution)/shard_map/ppermute | solution.py:322
  15.7 22.5 %collective-permute-start.24 = (bf16[3,64,128]{2,1,0:T(8,128)(2,1)S(1)}, bf16[3,64,128]{2,1,0:T(8,128)(2,1)S(1)}, u32[]{:S(2)}, u32[]{:S(2)}) collective-permute-start(bf16[3,64,128]{2,1,0:T(8,128)(2,1)S(1)} %get-tuple-element.968), channel_id=1, source_target_pairs={{0,4},{1,5},{2,6},{3,7},{4,0},{5,1},{6,2},{7,3},{8,12},{9,13},{10,... | collective-permute-start | bytes 147464 | tf_op jit(solution)/shard_map/ppermute | solution.py:322
  16.1 22.2 %collective-permute-start.23 = (bf16[3,64,128]{2,1,0:T(8,128)(2,1)S(1)}, bf16[3,64,128]{2,1,0:T(8,128)(2,1)S(1)}, u32[]{:S(2)}, u32[]{:S(2)}) collective-permute-start(bf16[3,64,128]{2,1,0:T(8,128)(2,1)S(1)} %get-tuple-element.969), channel_id=1, source_target_pairs={{0,3},{1,2},{2,1},{3,0},{4,7},{5,6},{6,5},{7,4},{8,11},{9,10},{10,... | collective-permute-start | bytes 147464 | tf_op jit(solution)/shard_map/ppermute | solution.py:322
  26.9 16.1 %all-to-all-start.31 = ((bf16[16,3,16,256]{3,2,1,0:T(8,128)(2,1)}), bf16[16,3,16,256]{3,2,1,0:T(8,128)(2,1)S(1)}, u32[]{:S(2)}, u32[]{:S(2)}) async-start(bf16[16,3,16,256]{3,2,1,0:T(8,128)(2,1)} %bitcast.47), calls=%async_computation.31 | async-start | bytes 786432 | tf_op jit(solution)/shard_map/all_to_all | solution.py:348
  33.4 4.8 %collective-permute-start.22 = (bf16[3,64,128]{2,1,0:T(8,128)(2,1)S(1)}, bf16[3,64,128]{2,1,0:T(8,128)(2,1)S(1)}, u32[]{:S(2)}, u32[]{:S(2)}) collective-permute-start(bf16[3,64,128]{2,1,0:T(8,128)(2,1)S(1)} %get-tuple-element.970), channel_id=1, source_target_pairs={{0,2},{1,3},{2,0},{3,1},{4,6},{5,7},{6,4},{7,5},{8,10},{9,11},{10,... | collective-permute-start | bytes 147464 | tf_op jit(solution)/shard_map/ppermute | solution.py:322
  35.3 2.9 %collective-permute-start.21 = (bf16[3,64,128]{2,1,0:T(8,128)(2,1)S(1)}, bf16[3,64,128]{2,1,0:T(8,128)(2,1)S(1)}, u32[]{:S(2)}, u32[]{:S(2)}) collective-permute-start(bf16[3,64,128]{2,1,0:T(8,128)(2,1)S(1)} %get-tuple-element.971), channel_id=1, source_target_pairs={{0,1},{1,0},{2,3},{3,2},{4,5},{5,4},{6,7},{7,6},{8,9},{9,8},{10,11... | collective-permute-start | bytes 147464 | tf_op jit(solution)/shard_map/ppermute | solution.py:322
  36.7 16.1 %collective-permute-start.20 = (s32[1,2]{1,0:T(1,128)S(1)}, s32[1,2]{1,0:T(1,128)S(1)}, u32[]{:S(2)}, u32[]{:S(2)}) collective-permute-start(s32[1,2]{1,0:T(1,128)S(1)} %add_bitcast_fusion), channel_id=1, source_target_pairs={{0,16},{16,0},{1,17},{17,1},{2,18},{18,2},{3,19},{19,3},{4,20},{20... | collective-permute-start | bytes 32 | tf_op jit(solution)/shard_map/ppermute | solution.py:378
  47.1 23.6 %all-to-all-start.32 = ((bf16[8,3,64,512]{3,2,1,0:T(8,128)(2,1)}), bf16[8,3,64,512]{3,2,1,0:T(8,128)(2,1)S(1)}, u32[]{:S(2)}, u32[]{:S(2)}) async-start(bf16[8,3,64,512]{3,2,1,0:T(8,128)(2,1)} %shard_map.110), calls=%async_computation.32 | async-start | bytes 3145728 | tf_op jit(solution)/shard_map/all_to_all | solution.py:319
  71.2 3.7 %copy-start.17 = (bf16[24,64,512]{2,1,0:T(8,128)(2,1)}, bf16[24,64,512]{2,1,0:T(8,128)(2,1)S(1)}, u32[]{:S(2)}) copy-start(bf16[24,64,512]{2,1,0:T(8,128)(2,1)S(1)} %get-tuple-element.494.refs_0_) | copy-start | bytes 4718596 | tf_op jit(solution)/shard_map/cond
  71.2 37.6 %all-to-all-start.3 = ((bf16[8,3,64,512]{3,2,1,0:T(8,128)(2,1)}), bf16[8,3,64,512]{3,2,1,0:T(8,128)(2,1)S(1)}, u32[]{:S(2)}, u32[]{:S(2)}) async-start(bf16[8,3,64,512]{3,2,1,0:T(8,128)(2,1)} %get-tuple-element.489), calls=%async_computation.3 | async-start | bytes 3145728 | tf_op jit(solution)/shard_map/cond/branch_3_fun/all_to_all | solution.py:319
  76.6 33.8 %collective-permute-start.2 = (bf16[10,64,512]{2,1,0:T(8,128)(2,1)}, bf16[10,64,512]{2,1,0:T(8,128)(2,1)S(1)}, u32[]{:S(2)}, u32[]{:S(2)}) collective-permute-start(bf16[10,64,512]{2,1,0:T(8,128)(2,1)} %branch_3_fun.6), channel_id=1, source_target_pairs={{0,8},{1,9},{2,10},{3,11},{4,12},{5,13},{6,14},{7,15},{8,0},{9,1},... | collective-permute-start | bytes 1966088 | tf_op jit(solution)/shard_map/cond/branch_3_fun/ppermute | solution.py:438
  108.9 1.8 copy-start.18
  110.4 38.1 %collective-permute-start.3 = (bf16[10,64,640]{2,1,0:T(8,128)(2,1)S(1)}, bf16[10,64,640]{2,1,0:T(8,128)(2,1)}, u32[]{:S(2)}, u32[]{:S(2)}) collective-permute-start(bf16[10,64,640]{2,1,0:T(8,128)(2,1)S(1)} %branch_3_fun.7), channel_id=1, source_target_pairs={{0,8},{1,9},{2,10},{3,11},{4,12},{5,13},{6,14},{7,15},{8,0},{9,1},... | collective-permute-start | bytes 2457608 | tf_op jit(solution)/shard_map/cond/branch_3_fun/ppermute | solution.py:441
  113.4 35.1 %copy-start.30 = (bf16[24,64,128]{2,1,0:T(8,128)(2,1)S(1)}, bf16[24,64,128]{2,1,0:T(8,128)(2,1)}, u32[]{:S(2)}) copy-start(bf16[24,64,128]{2,1,0:T(8,128)(2,1)} %get-tuple-element.490.refs_1_) | copy-start | bytes 1179652 | tf_op jit(solution)/shard_map/cond
  113.4 47.7 %all-to-all-start.5 = ((bf16[8,4,64,512]{3,2,1,0:T(8,128)(2,1)}), bf16[8,4,64,512]{3,2,1,0:T(8,128)(2,1)}, u32[]{:S(2)}, u32[]{:S(2)}) async-start(bf16[8,4,64,512]{3,2,1,0:T(8,128)(2,1)} %bitcast.15), calls=%async_computation.5 | async-start | bytes 4194304 | tf_op jit(solution)/shard_map/cond/branch_3_fun/all_to_all | solution.py:319
  161.1 34.9 %all-to-all-start.4 = ((bf16[8,4,64,640]{3,2,1,0:T(8,128)(2,1)}), bf16[8,4,64,640]{3,2,1,0:T(8,128)(2,1)S(1)}, u32[]{:S(2)}, u32[]{:S(2)}) async-start(bf16[8,4,64,640]{3,2,1,0:T(8,128)(2,1)} %bitcast.125), calls=%async_computation.4 | async-start | bytes 5242880 | tf_op jit(solution)/shard_map/cond/branch_3_fun/all_to_all | solution.py:319
  (1 other events, 1.5 us)
